TPU v7x, 32 devices: a whole 2x2x4 slice. The times are simulated.
32 devices in a mesh: subj: 2 (over x), row: 8 (over z, y), col: 2 (over core).
Axes of the slice: x: 2, y: 2, z: 4, core: 2. Of those that a mesh axis runs over, the one named last changes fastest.
Arguments:
- series: float32 [256, 11392], P(('subj', 'row', 'col')), parts along dimension 0, may hold values from -30 to 30
- tap_values: float32 [17], replicated, may hold values from -4 to 4
- tap_count: int32 [1], replicated, may hold values from 4 to 8
- kept_frames: int32 [32], P('subj'), parts along dimension 0, may hold values from 1 to 8, 96 in all
- band_start: int32 [2], P('subj'), parts along dimension 0, may hold values from 0 to 7296
Outputs:
- fisher_band: bfloat16 [8192, 11392], P('subj', ('row', 'col')), parts along dimension 0
There are 2 independent parts, one for each index of `subj`. A program takes and returns all parts, laid end to end along the dimension named above; an argument that names none is the same for every part. Nothing has to cross between parts.
Inputs may be any that keep to these rules, and one draw needn't show every extreme that they name: `tap_count`: frames farther than this from the centre get no weight. Time block d holds frames d * 8 to (d + 1) * 8 - 1; only its first kept_frames[d] frames are kept. `band_start`: the 4096 band grayordinates lie inside the grid.
All inputs are finite; a program needn't handle non-finite values.
Results may differ from a plain program's by a relative error of at most 0.0031.
The roundings to bfloat16 on the way count: a program that leaves them out, or rounds other values in their place, can miss the bound.
Values may be sent and summed in bfloat16 or wider, within the bound.
A program may use at most 128 MiB of HBM per device.

v0:
```python
import functools

import jax
import jax.numpy as jnp
from jax import lax
from jax.experimental import pallas as pl
from jax.experimental.pallas import tpu as pltpu
from jax.sharding import PartitionSpec as P

B = 4096
EPSILON = 1e-06
CLIP_LIMIT = 0.999
LANES = 128
TILE = 128
MESH = pl.DeviceIdType.MESH


def filter_rows(taps_ref, count_ref, kept_ref, tile, block, reach):
    shape = (TILE, TILE + 2 * reach)
    frame = lax.broadcasted_iota(jnp.int32, shape, 0)
    offset = lax.broadcasted_iota(jnp.int32, shape, 1) - frame
    taps = 2 * reach + 1
    total, amount = jnp.float32(0.0), jnp.float32(0.0)
    for j in range(taps):
        active = (count_ref[0] >= abs(j - reach)).astype(jnp.float32)
        total = total + active * taps_ref[j]
        amount = amount + active
    centre = jnp.full(shape, total) / jnp.full(shape, amount)
    rows = jnp.zeros(shape, jnp.float32)
    for j in range(taps):
        active = (count_ref[0] >= abs(j - reach)).astype(jnp.float32)
        rows = jnp.where(offset == j, active * (taps_ref[j] - centre), rows)
    kept = jnp.zeros(shape, jnp.int32)
    per = TILE // block
    for b in range(per):
        kept = jnp.where(frame // block == b, kept_ref[tile * per + b], kept)
    return jnp.where(frame % block < kept, rows, 0.0)


def prepare(sizes, series_hbm, taps_hbm, count_hbm, kept_hbm, start_hbm, own_ref, stage_ref,
            weights_ref, series_ref, taps_ref, count_ref, kept_ref, start_ref, sems):
    n, width, reach = sizes
    block, grays = series_ref.shape
    wide = stage_ref.shape[-1]
    pairs = (
        (taps_hbm, taps_ref), (count_hbm, count_ref), (kept_hbm, kept_ref),
        (start_hbm, start_ref), (series_hbm, series_ref),
    )
    copies = [pltpu.make_async_copy(a, b, sems.at[i]) for i, (a, b) in enumerate(pairs)]
    for copy in copies:
        copy.start()
    for copy in copies[:-1]:
        copy.wait()
    for i in range(weights_ref.shape[0]):
        weights_ref[i] = filter_rows(taps_ref, count_ref, kept_ref, i, block, reach)
    copies[-1].wait()
    start = start_ref[0]
    base = jnp.minimum(start // LANES * LANES, grays - B - LANES)
    shift = start - base
    window = series_ref[:, pl.ds(pl.multiple_of(base, LANES), B + LANES)]
    lane = lax.broadcasted_iota(jnp.int32, (block, LANES), 1)
    back = (LANES - shift) % LANES
    turned = [
        pltpu.roll(window[:, k * LANES : (k + 1) * LANES], back, 1) for k in range(B // LANES + 1)
    ]
    piece = own_ref.shape[-1]
    for k in range(B // LANES):
        at = k * LANES
        own_ref[at // piece, :, at % piece : at % piece + LANES] = jnp.where(
            lane < LANES - shift, turned[k], turned[k + 1]
        )
    for p in range(n):
        first = p * width // LANES * LANES
        part = series_ref[:, first : min(first + wide + LANES, grays)]
        off = p * width - first
        if off:
            part = pltpu.roll(part, part.shape[1] - off, 1)
        stage_ref[p] = part[:, :wide]


def exchange(sizes, own_ref, stage_ref, weights_ref, band_ref, cols_ref, raw, cols, held,
             own_send, own_recv, cols_send, cols_recv, band_send, band_recv):
    n_row, n_col, low = sizes
    n = n_row * n_col
    high = n_row // low
    pieces, block, piece = own_ref.shape
    frames = n * block
    wide = stage_ref.shape[-1]
    subj, row, col = lax.axis_index("subj"), lax.axis_index("row"), lax.axis_index("col")
    me = row * n_col + col
    h, l = row // low, row % low

    def device(q):
        return (subj, q // n_col, q % n_col)

    barrier = pltpu.get_barrier_semaphore()

    def greet(k, carry):
        pl.semaphore_signal(barrier, inc=1, device_id=device((me + k) % n), device_id_type=MESH)
        return carry

    lax.fori_loop(1, n, greet, 0)
    owner = me < pieces

    @pl.when(owner)
    def _():
        raw[me + 1] = own_ref[me % pieces]

    cols[me + 1] = stage_ref[me]
    for margin in (0, n + 1):
        raw[margin] = jnp.zeros_like(raw[margin])
        cols[margin] = jnp.zeros_like(cols[margin])
    pl.semaphore_wait(barrier, n - 1)

    def own_copy(p, sender):
        return pltpu.make_async_remote_copy(
            src_ref=own_ref.at[p], dst_ref=raw.at[sender + 1], send_sem=own_send.at[p],
            recv_sem=own_recv.at[sender], device_id=device(p), device_id_type=MESH,
        )

    def cols_copy(p, sender):
        return pltpu.make_async_remote_copy(
            src_ref=stage_ref.at[p], dst_ref=cols.at[sender + 1], send_sem=cols_send.at[p],
            recv_sem=cols_recv.at[sender], device_id=device(p), device_id_type=MESH,
        )

    def own_start(k, carry):
        p = (me + k) % n

        @pl.when(p < pieces)
        def _():
            own_copy(p, me).start()

        return carry

    lax.fori_loop(1, n, own_start, 0)

    def cols_start(k, carry):
        cols_copy((me + k) % n, me).start()
        return carry

    lax.fori_loop(1, n, cols_start, 0)

    tiles = frames // TILE
    per = TILE // block
    chunk = held.shape[-1]

    def scaled(source, at):
        spread = jnp.zeros((1, chunk), jnp.float32)
        for i in range(tiles):
            x = source[i * per : (i + 1) * per + 2, :, at : at + chunk]
            masked = lax.dot_general(
                weights_ref[i], x.reshape((per + 2) * block, chunk), (((1,), (0,)), ((), ())),
                precision=lax.Precision.HIGHEST, preferred_element_type=jnp.float32,
            )
            spread = spread + jnp.sum(masked * masked, axis=0, keepdims=True)
            if tiles > 1:
                held[i * TILE : (i + 1) * TILE] = masked
        if tiles > 1:
            masked = held[...]
        return (masked * lax.rsqrt(spread + EPSILON)).astype(jnp.bfloat16)

    @pl.when(owner)
    def _():
        def own_wait(k, carry):
            own_copy(0, (me + k) % n).wait_recv()
            return carry

        lax.fori_loop(1, n, own_wait, 0)
        for at in range(0, piece, chunk):
            band_ref[me % pieces, :, at : at + chunk] = scaled(raw, at)

    started = []

    def band_copy(q, to, site):
        return pltpu.make_async_remote_copy(
            src_ref=band_ref.at[q], dst_ref=band_ref.at[q], send_sem=band_send.at[site],
            recv_sem=band_recv.at[q], device_id=device(to), device_id_type=MESH,
        )

    def send(q, to, ok):
        site = len(started)
        started.append((q, to, ok))

        @pl.when(ok & (q < pieces))
        def _():
            band_copy(q, to, site).start()

    def arrived(q, ok):
        @pl.when(ok & (q < pieces))
        def _():
            band_copy(q, (me + 1) % n, 0).wait_recv()

    def index(hh, ll, cc):
        return (hh * low + ll) * n_col + cc

    always = me >= 0

    def share(q, ok):
        for k in range(1, n_col):
            send(q, index(h, l, (col + k) % n_col), ok)

    def pass_on(q, ok, upward, downward):
        if upward:
            send(q, index(h + 1, l, col), ok & (h + 1 < high))
        if downward:
            send(q, index(h - 1, l, col), ok & (h > 0))
        for k in range(1, low):
            send(q, index(h, (l + k) % low, col), ok)
        share(q, ok)

    def across(hh, ok):
        for k in range(1, low):
            q = index(hh, (l + k) % low, col)
            arrived(q, ok)
            share(q, ok)

    pass_on(me, always, True, True)
    for s in range(high):
        if s < high - 1:
            below, above = h - 1 - s, h + 1 + s
            q = index(below, l, col)
            arrived(q, below >= 0)
            pass_on(q, below >= 0, True, False)
            q = index(above, l, col)
            arrived(q, above < high)
            pass_on(q, above < high, False, True)
        if s == 0:
            across(h, always)
        else:
            across(h - s, h - s >= 0)
            across(h + s, h + s < high)

    def cols_wait(k, carry):
        cols_copy(0, (me + k) % n).wait_recv()
        return carry

    lax.fori_loop(1, n, cols_wait, 0)
    for at in range(0, wide, chunk):
        cols_ref[:, at : at + chunk] = scaled(cols, at)

    for hh in range(high):
        for ll in range(low):
            for k in range(1, n_col):
                arrived(index(hh, ll, (col + k) % n_col), always)

    def sent(k, carry):
        p = (me + k) % n
        cols_copy(p, me).wait_send()

        @pl.when(p < pieces)
        def _():
            own_copy(p, me).wait_send()

        return carry

    lax.fori_loop(1, n, sent, 0)
    for site, (q, to, ok) in enumerate(started):
        @pl.when(ok & (q < pieces))
        def _(site=site, q=q, to=to):
            band_copy(q, to, site).wait_send()


def fisher_kernel(cols_ref, band_ref, out_ref):
    c = lax.dot_general(
        cols_ref[...], band_ref[...], (((0,), (0,)), ((), ())), preferred_element_type=jnp.float32
    )[: out_ref.shape[0]]
    c = jnp.clip(c, -CLIP_LIMIT, CLIP_LIMIT)
    out_ref[...] = (0.5 * (jnp.log(1.0 + c) - jnp.log(1.0 - c))).astype(out_ref.dtype)


def body(series, tap_values, tap_count, kept_frames, band_start):
    n_row, n_col = lax.axis_size("row"), lax.axis_size("col")
    n = n_row * n_col
    low = max(k for k in range(1, n_row + 1) if n_row % k == 0 and k * k <= n_row)
    block, grays = series.shape
    width = grays // n
    wide = -(-width // 256) * 256
    reach = tap_values.shape[0] // 2
    frames = n * block
    high = n_row // low
    sites = (2 + low) + (high - 1) * 2 * (1 + low) + 2 * high * low
    pieces = min(n, B // LANES)
    piece = B // pieces
    chunk = min(piece, 256)
    tiles = frames // TILE
    anywhere = pl.BlockSpec(memory_space=pltpu.HBM)
    vmem = pl.BlockSpec(memory_space=pltpu.VMEM)
    f32, i32, bf16 = jnp.float32, jnp.int32, jnp.bfloat16
    own, stage, weights = pl.pallas_call(
        functools.partial(prepare, (n, width, reach)),
        out_shape=[
            jax.ShapeDtypeStruct((pieces, block, piece), f32),
            jax.ShapeDtypeStruct((n, block, wide), f32),
            jax.ShapeDtypeStruct((tiles, TILE, TILE + 2 * reach), f32),
        ],
        in_specs=[anywhere] * 5,
        out_specs=[vmem] * 3,
        scratch_shapes=[
            pltpu.VMEM(series.shape, f32),
            pltpu.SMEM(tap_values.shape, f32),
            pltpu.SMEM(tap_count.shape, i32),
            pltpu.SMEM(kept_frames.shape, i32),
            pltpu.SMEM(band_start.shape, i32),
            pltpu.SemaphoreType.DMA((5,)),
        ],
        compiler_params=pltpu.CompilerParams(vmem_limit_bytes=32 * 1024 * 1024),
    )(series, tap_values, tap_count, kept_frames, band_start)
    band, cols = pl.pallas_call(
        functools.partial(exchange, (n_row, n_col, low)),
        out_shape=[
            jax.ShapeDtypeStruct((pieces, frames, piece), bf16),
            jax.ShapeDtypeStruct((frames, wide), bf16),
        ],
        in_specs=[vmem] * 3,
        out_specs=[vmem] * 2,
        scratch_shapes=[
            pltpu.VMEM((n + 2, block, piece), f32),
            pltpu.VMEM((n + 2, block, wide), f32),
            pltpu.VMEM((frames, chunk), f32),
            pltpu.SemaphoreType.DMA((n,)),
            pltpu.SemaphoreType.DMA((n,)),
            pltpu.SemaphoreType.DMA((n,)),
            pltpu.SemaphoreType.DMA((n,)),
            pltpu.SemaphoreType.DMA((sites,)),
            pltpu.SemaphoreType.DMA((n,)),
        ],
        compiler_params=pltpu.CompilerParams(
            collective_id=0, has_side_effects=True, vmem_limit_bytes=40 * 1024 * 1024
        ),
    )(own, stage, weights)
    out = pl.pallas_call(
        fisher_kernel,
        grid=(pieces,),
        out_shape=jax.ShapeDtypeStruct((width, B), bf16),
        in_specs=[
            pl.BlockSpec((frames, wide), lambda i: (0, 0)),
            pl.BlockSpec((None, frames, piece), lambda i: (i, 0, 0)),
        ],
        out_specs=pl.BlockSpec((width, piece), lambda i: (0, i)),
        compiler_params=pltpu.CompilerParams(vmem_limit_bytes=32 * 1024 * 1024),
    )(cols, band)
    return out.T


def solution(mesh):
    placed = (P(("subj", "row", "col"), None), P(), P(), P("subj"), P("subj"))
    return jax.shard_map(
        body, mesh=mesh, in_specs=placed, out_specs=P("subj", ("row", "col")), check_vma=False
    )
```

profile of v0, /device:TPU:0, one launch (start us, length us, event | category | flops | bytes accessed | tf_op | source)
XLA Modules:
  0.0 46.4 jit_solution(4078654531308559891)
XLA Ops:
  1.3 0.0 copy-start
  1.3 1.0 %copy-done = f32[8,11392]{1,0:T(8,128)S(1)} copy-done((f32[8,11392]{1,0:T(8,128)S(1)}, f32[8,11392]{1,0:T(8,128)}, u32[]{:S(2)}) %copy-start) | copy-done | bytes 364568
  2.3 0.0 copy-start.1
  2.3 0.7 %copy-done.1 = f32[17]{0:T(128)S(1)} copy-done((f32[17]{0:T(128)S(1)}, f32[17]{0:T(128)}, u32[]{:S(2)}) %copy-start.1) | copy-done | bytes 92
  2.9 0.0 copy-start.2
  2.9 0.7 %copy-done.2 = s32[16]{0:T(128)S(1)} copy-done((s32[16]{0:T(128)S(1)}, s32[16]{0:T(128)}, u32[]{:S(2)}) %copy-start.2) | copy-done | bytes 88
  3.6 1.0 %shard_map.55 = (f32[16,8,256]{2,1,0:T(8,128)S(1)}, f32[16,8,768]{2,1,0:T(8,128)S(1)}, f32[1,128,144]{2,1,0:T(8,128)S(1)}) custom-call(f32[8,11392]{1,0:T(8,128)S(1)} %copy-done, f32[17]{0:T(128)S(1)} %copy-done.1, s32[1]{0:T(128)S(6)} %copy.6.count_hbm, s32[16]{0:T(128)S(1)} %copy-done.2, s32[1]{0:T(128)S(6)} %copy.7.start_hbm), custom_call_target="tpu_custom_call" | custom-call | tf_op jit(solution)/shard_map/pallas_call | solution.py:290
  4.6 32.1 %shard_map.56 = (bf16[16,128,256]{2,1,0:T(8,128)(2,1)S(1)}, bf16[128,768]{1,0:T(8,128)(2,1)S(1)}) custom-call(f32[16,8,256]{2,1,0:T(8,128)S(1)} %get-tuple-element.10.own_ref, f32[16,8,768]{2,1,0:T(8,128)S(1)} %get-tuple-element.11.stage_ref, f32[1,128,144]{2,1,0:T(8,128)S(1)} %get-tuple-element.12.weights_ref), custom_call_target="tpu_custom_call" | custom-call | tf_op jit(solution)/shard_map/pallas_call | solution.py:309
  36.7 9.7 %shard_map.57 = bf16[712,4096]{1,0:T(8,128)(2,1)} custom-call(bf16[128,768]{1,0:T(8,128)(2,1)S(1)} %get-tuple-element.13.cols_ref, bf16[16,128,256]{2,1,0:T(8,128)(2,1)S(1)} %get-tuple-element.14.band_ref), custom_call_target="tpu_custom_call" | custom-call | tf_op jit(solution)/shard_map/pallas_call | solution.py:332
Async XLA Ops:
  1.3 1.0 %copy-start = (f32[8,11392]{1,0:T(8,128)S(1)}, f32[8,11392]{1,0:T(8,128)}, u32[]{:S(2)}) copy-start(f32[8,11392]{1,0:T(8,128)} %series_hbm.1) | copy-start | bytes 1093636
  2.3 0.7 %copy-start.1 = (f32[17]{0:T(128)S(1)}, f32[17]{0:T(128)}, u32[]{:S(2)}) copy-start(f32[17]{0:T(128)} %taps_hbm.1) | copy-start | bytes 208
  2.9 0.7 %copy-start.2 = (s32[16]{0:T(128)S(1)}, s32[16]{0:T(128)}, u32[]{:S(2)}) copy-start(s32[16]{0:T(128)} %kept_hbm.1) | copy-start | bytes 196
where the time goes:
time: 46.7 us; the launch traced here: 46.4 us
  Pallas kernels  42.7 us (91%)
  local copies, waits for them, and re-layouts  2.29 us (5%)
  between operations  1.32 us (3%)
    pallas_call x1, Pallas kernels, body(): pl.pallas_call(functools.partial(exchange, (n_row, n_col, low)), out_shap...  32.1 us
    pallas_call x1, Pallas kernels, body(): pl.pallas_call(fisher_kernel, grid=(pieces,), out_shape=jax.ShapeDtypeStr...  9.7 us
    unnamed x6, local copies, waits for them, and re-layouts  2.29 us
    pallas_call x1, Pallas kernels, body(): pl.pallas_call(functools.partial(prepare, (n, width, reach)), out_shape=[...  0.97 us

commit v1 on v0

--- a/solution.py
+++ b/solution.py
@@ -78,7 +78,7 @@
         stage_ref[p] = part[:, :wide]
 
 
-def exchange(sizes, own_ref, stage_ref, weights_ref, band_ref, cols_ref, raw, cols, held,
+def exchange(sizes, own_ref, stage_ref, weights_ref, out_ref, band_ref, turned, raw, cols, held,
              own_send, own_recv, cols_send, cols_recv, band_send, band_recv):
     n_row, n_col, low = sizes
     n = n_row * n_col
@@ -158,7 +158,7 @@
                 held[i * TILE : (i + 1) * TILE] = masked
         if tiles > 1:
             masked = held[...]
-        return (masked * lax.rsqrt(spread + EPSILON)).astype(jnp.bfloat16)
+        return masked * lax.rsqrt(spread + EPSILON)
 
     @pl.when(owner)
     def _():
@@ -168,7 +168,7 @@
 
         lax.fori_loop(1, n, own_wait, 0)
         for at in range(0, piece, chunk):
-            band_ref[me % pieces, :, at : at + chunk] = scaled(raw, at)
+            band_ref[me % pieces, :, at : at + chunk] = scaled(raw, at).astype(jnp.bfloat16)
 
     started = []
 
@@ -178,9 +178,10 @@
             recv_sem=band_recv.at[q], device_id=device(to), device_id_type=MESH,
         )
 
-    def send(q, to, ok):
+    def send(what):
         site = len(started)
-        started.append((q, to, ok))
+        started.append(what)
+        q, to, ok = what()
 
         @pl.when(ok & (q < pieces))
         def _():
@@ -194,42 +195,50 @@
     def index(hh, ll, cc):
         return (hh * low + ll) * n_col + cc
 
-    always = me >= 0
-
-    def share(q, ok):
+    def inside(hh):
+        return (hh >= 0) & (hh < high)
+
+    def share(hh, ll):
         for k in range(1, n_col):
-            send(q, index(h, l, (col + k) % n_col), ok)
-
-    def pass_on(q, ok, upward, downward):
+            send(lambda k=k: (
+                index(hh(), ll(), col), index(h, l, (col + k) % n_col), inside(hh())
+            ))
+
+    def pass_on(hh, upward, downward):
         if upward:
-            send(q, index(h + 1, l, col), ok & (h + 1 < high))
+            send(lambda: (
+                index(hh(), l, col), index(h + 1, l, col), inside(hh()) & (h + 1 < high)
+            ))
         if downward:
-            send(q, index(h - 1, l, col), ok & (h > 0))
+            send(lambda: (index(hh(), l, col), index(h - 1, l, col), inside(hh()) & (h > 0)))
         for k in range(1, low):
-            send(q, index(h, (l + k) % low, col), ok)
-        share(q, ok)
-
-    def across(hh, ok):
+            send(lambda k=k: (
+                index(hh(), l, col), index(h, (l + k) % low, col), inside(hh())
+            ))
+        share(hh, lambda: l)
+
+    def across(hh):
         for k in range(1, low):
-            q = index(hh, (l + k) % low, col)
-            arrived(q, ok)
-            share(q, ok)
-
-    pass_on(me, always, True, True)
-    for s in range(high):
+            arrived(index(hh(), (l + k) % low, col), inside(hh()))
+            share(hh, lambda k=k: (l + k) % low)
+
+    def line(s):
+        for hh, upward in ((lambda: h - 1 - s, True), (lambda: h + 1 + s, False)):
+            arrived(index(hh(), l, col), inside(hh()))
+            pass_on(hh, upward, not upward)
+
+    def step(s):
         if s < high - 1:
-            below, above = h - 1 - s, h + 1 + s
-            q = index(below, l, col)
-            arrived(q, below >= 0)
-            pass_on(q, below >= 0, True, False)
-            q = index(above, l, col)
-            arrived(q, above < high)
-            pass_on(q, above < high, False, True)
-        if s == 0:
-            across(h, always)
+            line(s)
+        if s == 1:
+            across(lambda: h)
         else:
-            across(h - s, h - s >= 0)
-            across(h + s, h + s < high)
+            across(lambda: h - s + 1)
+            across(lambda: h + s - 1)
+
+    pass_on(lambda: h, True, True)
+    if high > 1:
+        line(0)
 
     def cols_wait(k, carry):
         cols_copy(0, (me + k) % n).wait_recv()
@@ -237,12 +246,39 @@
 
     lax.fori_loop(1, n, cols_wait, 0)
     for at in range(0, wide, chunk):
-        cols_ref[:, at : at + chunk] = scaled(cols, at)
-
-    for hh in range(high):
-        for ll in range(low):
-            for k in range(1, n_col):
-                arrived(index(hh, ll, (col + k) % n_col), always)
+        turned[at : at + chunk] = scaled(cols, at).T.astype(jnp.bfloat16)
+
+    near = low * n_col
+    rest = (high - 1) * low
+
+    def fisher(i, carry):
+        for s in range(1, high + 1):
+            @pl.when(i == s)
+            def _(s=s):
+                step(s)
+
+        j = jnp.maximum(i - near, 0)
+        far = i >= near
+        hh = jnp.where(far, (h + 1 + j % max(rest, 1) // low) % high, h)
+        ll = jnp.where(far, j % low, (l + i // n_col) % low)
+        cc = (col + jnp.where(far, j // max(rest, 1), i % n_col)) % n_col
+        q = index(hh, ll, cc)
+        arrived(q, cc != col)
+
+        @pl.when(q < pieces)
+        def _():
+            c = lax.dot_general(
+                turned[...], band_ref[q % pieces], (((1,), (0,)), ((), ())),
+                preferred_element_type=jnp.float32,
+            )[: out_ref.shape[0]]
+            c = jnp.clip(c, -CLIP_LIMIT, CLIP_LIMIT)
+            z = 0.5 * (jnp.log(1.0 + c) - jnp.log(1.0 - c))
+            at = pl.multiple_of(q % pieces * piece, piece)
+            out_ref[:, pl.ds(at, piece)] = z.astype(out_ref.dtype)
+
+        return carry
+
+    lax.fori_loop(0, n, fisher, 0)
 
     def sent(k, carry):
         p = (me + k) % n
@@ -255,18 +291,23 @@
         return carry
 
     lax.fori_loop(1, n, sent, 0)
-    for site, (q, to, ok) in enumerate(started):
+    for site, what in enumerate(started):
+        q, to, ok = what()
+
         @pl.when(ok & (q < pieces))
         def _(site=site, q=q, to=to):
             band_copy(q, to, site).wait_send()
 
 
-def fisher_kernel(cols_ref, band_ref, out_ref):
-    c = lax.dot_general(
-        cols_ref[...], band_ref[...], (((0,), (0,)), ((), ())), preferred_element_type=jnp.float32
-    )[: out_ref.shape[0]]
-    c = jnp.clip(c, -CLIP_LIMIT, CLIP_LIMIT)
-    out_ref[...] = (0.5 * (jnp.log(1.0 + c) - jnp.log(1.0 - c))).astype(out_ref.dtype)
+def store(value_ref, out_hbm, sems):
+    step = out_hbm.shape[1] // sems.shape[0]
+    copies = []
+    for i in range(sems.shape[0]):
+        part = (slice(None), slice(i * step, (i + 1) * step))
+        copies.append(pltpu.make_async_copy(value_ref.at[part], out_hbm.at[part], sems.at[i]))
+        copies[-1].start()
+    for copy in copies:
+        copy.wait()
 
 
 def body(series, tap_values, tap_count, kept_frames, band_start):
@@ -306,15 +347,14 @@
         ],
         compiler_params=pltpu.CompilerParams(vmem_limit_bytes=32 * 1024 * 1024),
     )(series, tap_values, tap_count, kept_frames, band_start)
-    band, cols = pl.pallas_call(
+    out = pl.pallas_call(
         functools.partial(exchange, (n_row, n_col, low)),
-        out_shape=[
-            jax.ShapeDtypeStruct((pieces, frames, piece), bf16),
-            jax.ShapeDtypeStruct((frames, wide), bf16),
-        ],
+        out_shape=jax.ShapeDtypeStruct((width, B), bf16),
         in_specs=[vmem] * 3,
-        out_specs=[vmem] * 2,
+        out_specs=vmem,
         scratch_shapes=[
+            pltpu.VMEM((pieces, frames, piece), bf16),
+            pltpu.VMEM((wide, frames), bf16),
             pltpu.VMEM((n + 2, block, piece), f32),
             pltpu.VMEM((n + 2, block, wide), f32),
             pltpu.VMEM((frames, chunk), f32),
@@ -330,16 +370,13 @@
         ),
     )(own, stage, weights)
     out = pl.pallas_call(
-        fisher_kernel,
-        grid=(pieces,),
+        store,
         out_shape=jax.ShapeDtypeStruct((width, B), bf16),
-        in_specs=[
-            pl.BlockSpec((frames, wide), lambda i: (0, 0)),
-            pl.BlockSpec((None, frames, piece), lambda i: (i, 0, 0)),
-        ],
-        out_specs=pl.BlockSpec((width, piece), lambda i: (0, i)),
+        in_specs=[vmem],
+        out_specs=anywhere,
+        scratch_shapes=[pltpu.SemaphoreType.DMA((4,))],
         compiler_params=pltpu.CompilerParams(vmem_limit_bytes=32 * 1024 * 1024),
-    )(cols, band)
+    )(out)
     return out.T
 
 

time: 46.7 us -> 44.6 us (0.955)
  Pallas kernels: 42.7 us -> 40.8 us
    pallas_call x1, Pallas kernels: 9.7 us -> 2.58 us  [body(): pl.pallas_call(store, out_shape=jax.ShapeDtypeStruct((width, B), bf16), i...]
    pallas_call x1, Pallas kernels: 32.1 us -> 37.3 us  [body(): pl.pallas_call(functools.partial(exchange, (n_row, n_col, low)), out_shap...]
where the time goes in v1:
time: 44.6 us; the launch traced here: 44.4 us
  Pallas kernels  40.8 us (91%)
  local copies, waits for them, and re-layouts  2.29 us (5%)
  between operations  1.32 us (3%)
    pallas_call x1, Pallas kernels, body(): pl.pallas_call(functools.partial(exchange, (n_row, n_col, low)), out_shap...  37.3 us
    pallas_call x1, Pallas kernels, body(): pl.pallas_call(store, out_shape=jax.ShapeDtypeStruct((width, B), bf16), i...  2.58 us
    unnamed x6, local copies, waits for them, and re-layouts  2.29 us
    pallas_call x1, Pallas kernels, body(): pl.pallas_call(functools.partial(prepare, (n, width, reach)), out_shape=[...  0.97 us

profile of v1, /device:TPU:0, one launch (start us, length us, event | category | flops | bytes accessed | tf_op | source)
XLA Modules:
  0.0 44.4 jit_solution(17744457210562181362)
XLA Ops:
  1.3 0.0 copy-start
  1.3 1.0 %copy-done = f32[8,11392]{1,0:T(8,128)S(1)} copy-done((f32[8,11392]{1,0:T(8,128)S(1)}, f32[8,11392]{1,0:T(8,128)}, u32[]{:S(2)}) %copy-start) | copy-done | bytes 364568
  2.3 0.0 copy-start.1
  2.3 0.7 %copy-done.1 = f32[17]{0:T(128)S(1)} copy-done((f32[17]{0:T(128)S(1)}, f32[17]{0:T(128)}, u32[]{:S(2)}) %copy-start.1) | copy-done | bytes 92
  2.9 0.0 copy-start.2
  2.9 0.7 %copy-done.2 = s32[16]{0:T(128)S(1)} copy-done((s32[16]{0:T(128)S(1)}, s32[16]{0:T(128)}, u32[]{:S(2)}) %copy-start.2) | copy-done | bytes 88
  3.6 1.0 %shard_map.55 = (f32[16,8,256]{2,1,0:T(8,128)S(1)}, f32[16,8,768]{2,1,0:T(8,128)S(1)}, f32[1,128,144]{2,1,0:T(8,128)S(1)}) custom-call(f32[8,11392]{1,0:T(8,128)S(1)} %copy-done, f32[17]{0:T(128)S(1)} %copy-done.1, s32[1]{0:T(128)S(6)} %copy.6.count_hbm, s32[16]{0:T(128)S(1)} %copy-done.2, s32[1]{0:T(128)S(6)} %copy.7.start_hbm), custom_call_target="tpu_custom_call" | custom-call | tf_op jit(solution)/shard_map/pallas_call | solution.py:331
  4.6 37.3 %shard_map.56.value_ref = bf16[712,4096]{1,0:T(8,128)(2,1)S(1)} custom-call(f32[16,8,256]{2,1,0:T(8,128)S(1)} %get-tuple-element.8.own_ref, f32[16,8,768]{2,1,0:T(8,128)S(1)} %get-tuple-element.9.stage_ref, f32[1,128,144]{2,1,0:T(8,128)S(1)} %get-tuple-element.10.weights_ref), custom_call_target="tpu_custom_call" | custom-call | tf_op jit(solution)/shard_map/pallas_call | solution.py:350
  41.8 2.6 %shard_map.57 = bf16[712,4096]{1,0:T(8,128)(2,1)} custom-call(bf16[712,4096]{1,0:T(8,128)(2,1)S(1)} %shard_map.56.value_ref), custom_call_target="tpu_custom_call" | custom-call | tf_op jit(solution)/shard_map/pallas_call | solution.py:372
Async XLA Ops:
  1.3 1.0 %copy-start = (f32[8,11392]{1,0:T(8,128)S(1)}, f32[8,11392]{1,0:T(8,128)}, u32[]{:S(2)}) copy-start(f32[8,11392]{1,0:T(8,128)} %series_hbm.1) | copy-start | bytes 1093636
  2.3 0.7 %copy-start.1 = (f32[17]{0:T(128)S(1)}, f32[17]{0:T(128)}, u32[]{:S(2)}) copy-start(f32[17]{0:T(128)} %taps_hbm.1) | copy-start | bytes 208
  2.9 0.7 %copy-start.2 = (s32[16]{0:T(128)S(1)}, s32[16]{0:T(128)}, u32[]{:S(2)}) copy-start(s32[16]{0:T(128)} %kept_hbm.1) | copy-start | bytes 196

commit v2 on v1

--- a/solution.py
+++ b/solution.py
@@ -37,11 +37,12 @@
     return jnp.where(frame % block < kept, rows, 0.0)
 
 
-def prepare(sizes, series_hbm, taps_hbm, count_hbm, kept_hbm, start_hbm, own_ref, stage_ref,
+def prepare(sizes, series_hbm, taps_hbm, count_hbm, kept_hbm, start_hbm, stage_ref,
             weights_ref, series_ref, taps_ref, count_ref, kept_ref, start_ref, sems):
-    n, width, reach = sizes
+    n, width, pieces, piece, reach = sizes
     block, grays = series_ref.shape
-    wide = stage_ref.shape[-1]
+    plane = stage_ref.shape[0]
+    wide = stage_ref.shape[-1] - piece
     pairs = (
         (taps_hbm, taps_ref), (count_hbm, count_ref), (kept_hbm, kept_ref),
         (start_hbm, start_ref), (series_hbm, series_ref),
@@ -63,10 +64,10 @@
     turned = [
         pltpu.roll(window[:, k * LANES : (k + 1) * LANES], back, 1) for k in range(B // LANES + 1)
     ]
-    piece = own_ref.shape[-1]
     for k in range(B // LANES):
         at = k * LANES
-        own_ref[at // piece, :, at % piece : at % piece + LANES] = jnp.where(
+        p, to = at // piece, wide + at % piece
+        stage_ref[p % plane, p // plane, :, to : to + LANES] = jnp.where(
             lane < LANES - shift, turned[k], turned[k + 1]
         )
     for p in range(n):
@@ -75,80 +76,78 @@
         off = p * width - first
         if off:
             part = pltpu.roll(part, part.shape[1] - off, 1)
-        stage_ref[p] = part[:, :wide]
-
-
-def exchange(sizes, own_ref, stage_ref, weights_ref, out_ref, band_ref, turned, raw, cols, held,
-             own_send, own_recv, cols_send, cols_recv, band_send, band_recv):
+        stage_ref[p % plane, p // plane, :, :wide] = part[:, :wide]
+        if p >= pieces:
+            stage_ref[p % plane, p // plane, :, wide:] = jnp.zeros((block, piece), part.dtype)
+
+
+def exchange(sizes, stage_ref, weights_ref, out_ref, band_ref, turned, mid, raw, held,
+             plane_send, plane_recv, line_send, line_recv, band_send, band_recv):
     n_row, n_col, low = sizes
     n = n_row * n_col
     high = n_row // low
-    pieces, block, piece = own_ref.shape
-    frames = n * block
-    wide = stage_ref.shape[-1]
+    plane, _, block, _ = stage_ref.shape
+    pieces, frames, piece = band_ref.shape
+    wide = stage_ref.shape[-1] - piece
     subj, row, col = lax.axis_index("subj"), lax.axis_index("row"), lax.axis_index("col")
     me = row * n_col + col
     h, l = row // low, row % low
+    own = l * n_col + col
 
     def device(q):
         return (subj, q // n_col, q % n_col)
 
+    def beside(k):
+        return (own + k) % plane
+
+    def along(k):
+        return (h + k) % high
+
     barrier = pltpu.get_barrier_semaphore()
-
-    def greet(k, carry):
-        pl.semaphore_signal(barrier, inc=1, device_id=device((me + k) % n), device_id_type=MESH)
-        return carry
-
-    lax.fori_loop(1, n, greet, 0)
+    for k in range(1, plane):
+        pl.semaphore_signal(
+            barrier, inc=1, device_id=device(h * plane + beside(k)), device_id_type=MESH
+        )
+    for k in range(1, high):
+        pl.semaphore_signal(
+            barrier, inc=1, device_id=device(along(k) * plane + own), device_id_type=MESH
+        )
     owner = me < pieces
-
-    @pl.when(owner)
-    def _():
-        raw[me + 1] = own_ref[me % pieces]
-
-    cols[me + 1] = stage_ref[me]
+    mid[own] = stage_ref[own]
     for margin in (0, n + 1):
         raw[margin] = jnp.zeros_like(raw[margin])
-        cols[margin] = jnp.zeros_like(cols[margin])
-    pl.semaphore_wait(barrier, n - 1)
-
-    def own_copy(p, sender):
+    pl.semaphore_wait(barrier, plane + high - 2)
+
+    def plane_copy(to, sender):
         return pltpu.make_async_remote_copy(
-            src_ref=own_ref.at[p], dst_ref=raw.at[sender + 1], send_sem=own_send.at[p],
-            recv_sem=own_recv.at[sender], device_id=device(p), device_id_type=MESH,
-        )
-
-    def cols_copy(p, sender):
+            src_ref=stage_ref.at[to], dst_ref=mid.at[sender], send_sem=plane_send.at[to],
+            recv_sem=plane_recv.at[sender], device_id=device(h * plane + to),
+            device_id_type=MESH,
+        )
+
+    def line_copy(to, sender):
         return pltpu.make_async_remote_copy(
-            src_ref=stage_ref.at[p], dst_ref=cols.at[sender + 1], send_sem=cols_send.at[p],
-            recv_sem=cols_recv.at[sender], device_id=device(p), device_id_type=MESH,
-        )
-
-    def own_start(k, carry):
-        p = (me + k) % n
-
-        @pl.when(p < pieces)
-        def _():
-            own_copy(p, me).start()
-
-        return carry
-
-    lax.fori_loop(1, n, own_start, 0)
-
-    def cols_start(k, carry):
-        cols_copy((me + k) % n, me).start()
-        return carry
-
-    lax.fori_loop(1, n, cols_start, 0)
+            src_ref=mid.at[:, to], dst_ref=raw.at[pl.ds(sender * plane + 1, plane)],
+            send_sem=line_send.at[to], recv_sem=line_recv.at[sender],
+            device_id=device(to * plane + own), device_id_type=MESH,
+        )
+
+    for k in range(1, plane):
+        plane_copy(beside(k), own).start()
+    for k in range(1, plane):
+        plane_copy(beside(k), beside(k)).wait_recv()
+    for k in range(1, high):
+        line_copy(along(k), h).start()
+    raw[pl.ds(h * plane + 1, plane)] = mid[:, h]
 
     tiles = frames // TILE
     per = TILE // block
     chunk = held.shape[-1]
 
-    def scaled(source, at):
+    def scaled(at):
         spread = jnp.zeros((1, chunk), jnp.float32)
         for i in range(tiles):
-            x = source[i * per : (i + 1) * per + 2, :, at : at + chunk]
+            x = raw[i * per : (i + 1) * per + 2, :, at : at + chunk]
             masked = lax.dot_general(
                 weights_ref[i], x.reshape((per + 2) * block, chunk), (((1,), (0,)), ((), ())),
                 precision=lax.Precision.HIGHEST, preferred_element_type=jnp.float32,
@@ -160,15 +159,13 @@
             masked = held[...]
         return masked * lax.rsqrt(spread + EPSILON)
 
+    for k in range(1, high):
+        line_copy(along(k), along(k)).wait_recv()
+
     @pl.when(owner)
     def _():
-        def own_wait(k, carry):
-            own_copy(0, (me + k) % n).wait_recv()
-            return carry
-
-        lax.fori_loop(1, n, own_wait, 0)
         for at in range(0, piece, chunk):
-            band_ref[me % pieces, :, at : at + chunk] = scaled(raw, at).astype(jnp.bfloat16)
+            band_ref[me % pieces, :, at : at + chunk] = scaled(wide + at).astype(jnp.bfloat16)
 
     started = []
 
@@ -237,16 +234,10 @@
             across(lambda: h + s - 1)
 
     pass_on(lambda: h, True, True)
-    if high > 1:
-        line(0)
-
-    def cols_wait(k, carry):
-        cols_copy(0, (me + k) % n).wait_recv()
-        return carry
-
-    lax.fori_loop(1, n, cols_wait, 0)
     for at in range(0, wide, chunk):
-        turned[at : at + chunk] = scaled(cols, at).T.astype(jnp.bfloat16)
+        turned[at : at + chunk] = scaled(at).T.astype(jnp.bfloat16)
+        if at == 0 and high > 1:
+            line(0)
 
     near = low * n_col
     rest = (high - 1) * low
@@ -280,17 +271,10 @@
 
     lax.fori_loop(0, n, fisher, 0)
 
-    def sent(k, carry):
-        p = (me + k) % n
-        cols_copy(p, me).wait_send()
-
-        @pl.when(p < pieces)
-        def _():
-            own_copy(p, me).wait_send()
-
-        return carry
-
-    lax.fori_loop(1, n, sent, 0)
+    for k in range(1, plane):
+        plane_copy(beside(k), own).wait_send()
+    for k in range(1, high):
+        line_copy(along(k), h).wait_send()
     for site, what in enumerate(started):
         q, to, ok = what()
 
@@ -328,15 +312,15 @@
     anywhere = pl.BlockSpec(memory_space=pltpu.HBM)
     vmem = pl.BlockSpec(memory_space=pltpu.VMEM)
     f32, i32, bf16 = jnp.float32, jnp.int32, jnp.bfloat16
-    own, stage, weights = pl.pallas_call(
-        functools.partial(prepare, (n, width, reach)),
+    plane = low * n_col
+    stage, weights = pl.pallas_call(
+        functools.partial(prepare, (n, width, pieces, piece, reach)),
         out_shape=[
-            jax.ShapeDtypeStruct((pieces, block, piece), f32),
-            jax.ShapeDtypeStruct((n, block, wide), f32),
+            jax.ShapeDtypeStruct((plane, high, block, wide + piece), f32),
             jax.ShapeDtypeStruct((tiles, TILE, TILE + 2 * reach), f32),
         ],
         in_specs=[anywhere] * 5,
-        out_specs=[vmem] * 3,
+        out_specs=[vmem] * 2,
         scratch_shapes=[
             pltpu.VMEM(series.shape, f32),
             pltpu.SMEM(tap_values.shape, f32),
@@ -350,25 +334,25 @@
     out = pl.pallas_call(
         functools.partial(exchange, (n_row, n_col, low)),
         out_shape=jax.ShapeDtypeStruct((width, B), bf16),
-        in_specs=[vmem] * 3,
+        in_specs=[vmem] * 2,
         out_specs=vmem,
         scratch_shapes=[
             pltpu.VMEM((pieces, frames, piece), bf16),
             pltpu.VMEM((wide, frames), bf16),
-            pltpu.VMEM((n + 2, block, piece), f32),
-            pltpu.VMEM((n + 2, block, wide), f32),
+            pltpu.VMEM((plane, high, block, wide + piece), f32),
+            pltpu.VMEM((n + 2, block, wide + piece), f32),
             pltpu.VMEM((frames, chunk), f32),
-            pltpu.SemaphoreType.DMA((n,)),
-            pltpu.SemaphoreType.DMA((n,)),
-            pltpu.SemaphoreType.DMA((n,)),
-            pltpu.SemaphoreType.DMA((n,)),
+            pltpu.SemaphoreType.DMA((plane,)),
+            pltpu.SemaphoreType.DMA((plane,)),
+            pltpu.SemaphoreType.DMA((high,)),
+            pltpu.SemaphoreType.DMA((high,)),
             pltpu.SemaphoreType.DMA((sites,)),
             pltpu.SemaphoreType.DMA((n,)),
         ],
         compiler_params=pltpu.CompilerParams(
             collective_id=0, has_side_effects=True, vmem_limit_bytes=40 * 1024 * 1024
         ),
-    )(own, stage, weights)
+    )(stage, weights)
     out = pl.pallas_call(
         store,
         out_shape=jax.ShapeDtypeStruct((width, B), bf16),

time: 44.6 us -> 51.4 us (1.15)
  Pallas kernels: 40.8 us -> 47.6 us
    pallas_call x1, Pallas kernels: 37.3 us -> 44.1 us  [body(): pl.pallas_call(functools.partial(exchange, (n_row, n_col, low)), out_shap...]
where the time goes in v2:
time: 51.4 us; the launch traced here: 51.2 us
  Pallas kernels  47.6 us (93%)
  local copies, waits for them, and re-layouts  2.29 us (4%)
  between operations  1.32 us (3%)
    pallas_call x1, Pallas kernels, body(): pl.pallas_call(functools.partial(exchange, (n_row, n_col, low)), out_shap...  44.1 us
    pallas_call x1, Pallas kernels, body(): pl.pallas_call(store, out_shape=jax.ShapeDtypeStruct((width, B), bf16), i...  2.58 us
    unnamed x6, local copies, waits for them, and re-layouts  2.29 us

profile of v2, /device:TPU:0, one launch (start us, length us, event | category | flops | bytes accessed | tf_op | source)
XLA Modules:
  0.0 51.2 jit_solution(14387105729364208510)
XLA Ops:
  1.3 0.0 copy-start
  1.3 1.0 %copy-done = f32[8,11392]{1,0:T(8,128)S(1)} copy-done((f32[8,11392]{1,0:T(8,128)S(1)}, f32[8,11392]{1,0:T(8,128)}, u32[]{:S(2)}) %copy-start) | copy-done | bytes 364568
  2.3 0.0 copy-start.1
  2.3 0.7 %copy-done.1 = f32[17]{0:T(128)S(1)} copy-done((f32[17]{0:T(128)S(1)}, f32[17]{0:T(128)}, u32[]{:S(2)}) %copy-start.1) | copy-done | bytes 92
  2.9 0.0 copy-start.2
  2.9 0.7 %copy-done.2 = s32[16]{0:T(128)S(1)} copy-done((s32[16]{0:T(128)S(1)}, s32[16]{0:T(128)}, u32[]{:S(2)}) %copy-start.2) | copy-done | bytes 88
  3.6 1.0 %shard_map.55 = (f32[4,4,8,1024]{3,2,1,0:T(8,128)S(1)}, f32[1,128,144]{2,1,0:T(8,128)S(1)}) custom-call(f32[8,11392]{1,0:T(8,128)S(1)} %copy-done, f32[17]{0:T(128)S(1)} %copy-done.1, s32[1]{0:T(128)S(6)} %copy.6.count_hbm, s32[16]{0:T(128)S(1)} %copy-done.2, s32[1]{0:T(128)S(6)} %copy.7.start_hbm), custom_call_target="tpu_custom_call" | custom-call | tf_op jit(solution)/shard_map/pallas_call | solution.py:316
  4.6 44.1 %shard_map.56.value_ref = bf16[712,4096]{1,0:T(8,128)(2,1)S(1)} custom-call(f32[4,4,8,1024]{3,2,1,0:T(8,128)S(1)} %get-tuple-element.7.stage_ref, f32[1,128,144]{2,1,0:T(8,128)S(1)} %get-tuple-element.8.weights_ref), custom_call_target="tpu_custom_call" | custom-call | tf_op jit(solution)/shard_map/pallas_call | solution.py:334
  48.7 2.6 %shard_map.57 = bf16[712,4096]{1,0:T(8,128)(2,1)} custom-call(bf16[712,4096]{1,0:T(8,128)(2,1)S(1)} %shard_map.56.value_ref), custom_call_target="tpu_custom_call" | custom-call | tf_op jit(solution)/shard_map/pallas_call | solution.py:356
Async XLA Ops:
  1.3 1.0 %copy-start = (f32[8,11392]{1,0:T(8,128)S(1)}, f32[8,11392]{1,0:T(8,128)}, u32[]{:S(2)}) copy-start(f32[8,11392]{1,0:T(8,128)} %series_hbm.1) | copy-start | bytes 1093636
  2.3 0.7 %copy-start.1 = (f32[17]{0:T(128)S(1)}, f32[17]{0:T(128)}, u32[]{:S(2)}) copy-start(f32[17]{0:T(128)} %taps_hbm.1) | copy-start | bytes 208
  2.9 0.7 %copy-start.2 = (s32[16]{0:T(128)S(1)}, s32[16]{0:T(128)}, u32[]{:S(2)}) copy-start(s32[16]{0:T(128)} %kept_hbm.1) | copy-start | bytes 196
